TPU v7x, 512 devices: a whole 4x8x8 slice. The times are simulated.
512 devices in a mesh: row: 16 (over x_hi, y), col: 32 (over z, x_lo, core).
Axes of the slice: x: 4 (x_hi: 2, x_lo: 2; x = x_hi * 2 + x_lo), y: 8, z: 8, core: 2. Of those that a mesh axis runs over, the one named last changes fastest.
Arguments:
- density: float32 [4096, 4096], P('row', 'col'), may hold values from -1 to 1
- pattern: int32 [32, 32], P('row', 'col'), may hold values from 0 to 1, as said below
- keep_mask: int32 [32, 32], P('row', 'col'), may hold values from 0 to 1, as said below
Outputs:
- purified: float32 [4096, 4096], P('row', 'col')
Inputs may be any that keep to these rules, and one draw needn't show every extreme that they name: `pattern`: symmetric, with ones on the diagonal. `keep_mask`: symmetric, with ones on the diagonal.
All inputs are finite; a program needn't handle non-finite values.
Results may differ from a plain program's by a relative error of at most 0.00014.
Values sent between devices are 32-bit elements; how exact they have to be, the bound alone decides.
A program may use at most 64 MiB of HBM per device.

v0:
```python
import jax
import jax.numpy as jnp
from jax import lax
from jax.sharding import PartitionSpec as P

BLOCK = 128
STEPS = 2


def widen(mask, block):
    rows, cols = mask.shape
    full = jnp.broadcast_to(mask.astype(jnp.float32)[:, None, :, None], (rows, block, cols, block))
    return full.reshape(rows * block, cols * block)


def product(left, right):
    return jnp.dot(left, right, precision=lax.Precision.HIGHEST, preferred_element_type=jnp.float32)


def per_device(density, pattern, keep_mask):
    keep = widen(keep_mask, BLOCK)
    current = density * widen(pattern, BLOCK)
    for step in range(STEPS):
        panel = lax.all_gather(current, "col", axis=1, tiled=True)
        columns = lax.all_gather(current, "row", axis=0, tiled=True)
        square = keep * product(panel, columns)
        square_cols = lax.all_gather(square, "row", axis=0, tiled=True)
        cube = keep * product(panel, square_cols)
        current = 3.0 * square - 2.0 * cube
    return current


def solution(mesh):
    placed = (P("row", "col"), P("row", "col"), P("row", "col"))
    return jax.shard_map(
        per_device, mesh=mesh, in_specs=placed, out_specs=P("row", "col"), check_vma=False
    )
```

profile of v0, /device:TPU:1, one launch (start us, length us, event | category | flops | bytes accessed | tf_op | source)
XLA Modules:
  0.0 553.1 jit_solution(12773544341143343943)
XLA Ops:
  6.5 0.0 all-gather.9.cloned.1.call-start
  6.5 0.7 convert_bitcast_fusion
  7.2 0.1 broadcast_bitcast_fusion
  7.3 1.7 broadcast_multiply_fusion
  8.9 0.0 all-gather.9.cloned.1.call-update
  9.0 0.0 all-gather.7.cloned.1.call-start
  9.0 0.7 all-gather.7.cloned.1.call-update
  9.7 0.0 all-gather.11.cloned.1.call-start
  9.8 0.7 convert_bitcast_fusion.1
  10.4 0.1 broadcast_bitcast_fusion.1
  10.5 92.8 %all-gather.9.cloned.1.call-done = f32[4096,128]{1,0:T(8,128)} async-done(((f32[256,128]{1,0:T(8,128)}), f32[4096,128]{1,0:T(8,128)}) %all-gather.9.cloned.1.call-update) | async-done | bytes 2097168 | tf_op jit(solution)/shard_map/all_gather | solution.py:25
  103.3 78.5 %all-gather.7.cloned.1.call-done = f32[256,4096]{1,0:T(8,128)} async-done(((f32[256,128]{1,0:T(8,128)}), f32[256,4096]{1,0:T(8,128)}) %all-gather.7.cloned.1.call-update) | async-done | bytes 4194320 | tf_op jit(solution)/shard_map/all_gather | solution.py:24
  181.8 7.0 %convolution_multiply_fusion.3 = f32[256,128]{1,0:T(8,128)} fusion(f32[256,4096]{1,0:T(8,128)} %all-gather.7.cloned.1.call-done, f32[4096,128]{1,0:T(8,128)} %all-gather.9.cloned.1.call-done, f32[256]{0:T(256)S(1)} %broadcast_bitcast_fusion.1), kind=kOutput, calls=%fused_computation.7 | convolution fusion | flops 1610645504 | bytes 6423552 | tf_op jit(solution)/shard_map/dot_general | solution.py:17
  188.8 0.0 all-gather.11.cloned.1.call-update
  188.8 0.0 all-gather.15.cloned.1.call-start
  188.8 85.1 %all-gather.11.cloned.1.call-done = f32[4096,128]{1,0:T(8,128)} async-done(((f32[256,128]{1,0:T(8,128)}), f32[4096,128]{1,0:T(8,128)}) %all-gather.11.cloned.1.call-update) | async-done | bytes 2097168 | tf_op jit(solution)/shard_map/all_gather | solution.py:27
  273.9 6.9 %fusion.3 = f32[256,128]{1,0:T(8,128)} fusion(f32[256,4096]{1,0:T(8,128)} %all-gather.7.cloned.1.call-done, f32[4096,128]{1,0:T(8,128)} %all-gather.11.cloned.1.call-done, f32[256,128]{1,0:T(8,128)} %convolution_multiply_fusion.3, f32[256]{0:T(256)S(1)} %broadcast_bitcast_fusion.1), kind=kOutput, calls=%fused_computation.6 | convolution fusion | flops 1610743808 | bytes 6554624 | tf_op jit(solution)/shard_map/dot_general | solution.py:17
  280.9 0.0 all-gather.15.cloned.1.call-update
  280.9 0.0 all-gather.13.cloned.1.call-start
  281.0 0.5 all-gather.13.cloned.1.call-update
  281.5 0.2 all-gather.17.cloned.1.call-start
  281.7 87.0 %all-gather.15.cloned.1.call-done = f32[4096,128]{1,0:T(8,128)} async-done(((f32[256,128]{1,0:T(8,128)}), f32[4096,128]{1,0:T(8,128)}) %all-gather.15.cloned.1.call-update) | async-done | bytes 2097168 | tf_op jit(solution)/shard_map/all_gather | solution.py:25
  368.7 78.4 %all-gather.13.cloned.1.call-done = f32[256,4096]{1,0:T(8,128)} async-done(((f32[256,128]{1,0:T(8,128)}), f32[256,4096]{1,0:T(8,128)}) %all-gather.13.cloned.1.call-update) | async-done | bytes 4194320 | tf_op jit(solution)/shard_map/all_gather | solution.py:24
  447.1 7.0 %convolution_multiply_fusion.1 = f32[256,128]{1,0:T(8,128)} fusion(f32[256,4096]{1,0:T(8,128)} %all-gather.13.cloned.1.call-done, f32[4096,128]{1,0:T(8,128)} %all-gather.15.cloned.1.call-done, f32[256]{0:T(256)S(1)} %broadcast_bitcast_fusion.1), kind=kOutput, calls=%fused_computation.3 | convolution fusion | flops 1610645504 | bytes 6423552 | tf_op jit(solution)/shard_map/dot_general | solution.py:17
  454.1 0.0 all-gather.17.cloned.1.call-update
  454.1 85.2 %all-gather.17.cloned.1.call-done = f32[4096,128]{1,0:T(8,128)} async-done(((f32[256,128]{1,0:T(8,128)}), f32[4096,128]{1,0:T(8,128)}) %all-gather.17.cloned.1.call-update) | async-done | bytes 2097168 | tf_op jit(solution)/shard_map/all_gather | solution.py:27
  539.3 6.9 %fusion.1 = f32[256,128]{1,0:T(8,128)} fusion(f32[256,4096]{1,0:T(8,128)} %all-gather.13.cloned.1.call-done, f32[4096,128]{1,0:T(8,128)} %all-gather.17.cloned.1.call-done, f32[256,128]{1,0:T(8,128)} %convolution_multiply_fusion.1, f32[256]{0:T(256)S(1)} %broadcast_bitcast_fusion.1), kind=kOutput, calls=%fused_computation.2 | convolution fusion | flops 1610743808 | bytes 6554624 | tf_op jit(solution)/shard_map/dot_general | solution.py:17
Async XLA Ops:
  6.5 96.7 %all-gather.9.cloned.1.call-start = ((), (), s32[]{:S(2)}) async-start(), calls=%async_computation.1 | async-start | bytes 2228224 | tf_op jit(solution)/shard_map/all_gather | solution.py:25
  9.0 172.8 %all-gather.7.cloned.1.call-start = ((), (), s32[]{:S(2)}) async-start(), calls=%async_computation | async-start | bytes 4325376 | tf_op jit(solution)/shard_map/all_gather | solution.py:24
  9.7 264.2 %all-gather.11.cloned.1.call-start = ((), (), s32[]{:S(2)}) async-start(), calls=%async_computation.2 | async-start | bytes 2228224 | tf_op jit(solution)/shard_map/all_gather | solution.py:27
  188.8 180.0 %all-gather.15.cloned.1.call-start = ((), (), s32[]{:S(2)}) async-start(), calls=%async_computation.4 | async-start | bytes 2228224 | tf_op jit(solution)/shard_map/all_gather | solution.py:25
  280.9 166.2 %all-gather.13.cloned.1.call-start = ((), (), s32[]{:S(2)}) async-start(), calls=%async_computation.3 | async-start | bytes 4325376 | tf_op jit(solution)/shard_map/all_gather | solution.py:24
  281.5 257.8 %all-gather.17.cloned.1.call-start = ((), (), s32[]{:S(2)}) async-start(), calls=%async_computation.5 | async-start | bytes 2228224 | tf_op jit(solution)/shard_map/all_gather | solution.py:27
Sparse Core Ops, SparseCore 0:
  10.5 92.6 all-gather.8
  105.3 76.4 all-gather.6
  188.9 84.9 all-gather.10
  281.0 87.6 all-gather.14
  370.7 76.4 all-gather.12
  454.2 85.0 all-gather.16
where the time goes:
time: 556 us; the launch traced here: 553 us
  waiting for transfers between devices  508 us (91%)
  matrix products  27.8 us (5%)
  between operations  13.5 us (2%)
    all_gather x2, waiting for transfers between devices, per_device(): columns = lax.all_gather(current, 'row', axis=0, tiled=True)  180 us
    all_gather x2, waiting for transfers between devices, per_device(): square_cols = lax.all_gather(square, 'row', axis=0, tiled=True)  170 us
    all_gather x2, waiting for transfers between devices, per_device(): panel = lax.all_gather(current, 'col', axis=1, tiled=True)  157 us
    dot_general x4, matrix products, product(): jnp.dot(left, right, precision=lax.Precision.HIGHEST, preferred_element_t...  27.8 us
  transfers between devices with their start and end apart: 6, of which 6 were waited for; matrix products, arithmetic and copies ran while one was open for 0% of the time, Pallas kernels for 0%

commit v1 on v0

v1 whole, which is shorter than its diff:
```python
import functools

import jax
import jax.numpy as jnp
from jax import lax
from jax.experimental import pallas as pl
from jax.experimental.pallas import tpu as pltpu
from jax.sharding import PartitionSpec as P

STEPS = 2
NX, NY, NZ = 4, 8, 8
ROWS, COLS = 256, 128
GROUPS = 16
CUT = 128
MESH = pl.DeviceIdType.MESH


def place(x, y, z, c):
    return ((x // 2) * NY + y, z * 4 + (x % 2) * 2 + c)


def slot(x, z):
    return z * 4 + (x % 2) * 2 + x // 2


def arrived(ref, sem):
    pltpu.make_async_copy(ref, ref, sem).wait()


def kernel(
    density, pattern, keep_mask, out,
    message, own, panel, column, left, right, total, square, answer, reply,
    swap_sems, panel_sems, column_sems, send_sems,
):
    row, col = lax.axis_index("row"), lax.axis_index("col")
    y, z, c = row % NY, col // 4, col % 2
    h, l = row // NY, (col // 2) % 2
    x = h * 2 + l

    def at(dx=0, dy=0, dz=0, core=None):
        return place(
            (x + dx + NX) % NX, (y + dy + NY) % NY, (z + dz + NZ) % NZ, c if core is None else core
        )

    sibling = at(core=1 - c)
    across = at(dx=2, core=1 - c)
    swaps = h != c
    barrier = pltpu.get_barrier_semaphore()
    friends = [
        at(dx=1), at(dx=-1), at(dx=2), at(dy=1), at(dy=-1), at(dz=1), at(dz=-1), sibling, across,
    ]
    for friend in friends:
        pl.semaphore_signal(barrier, inc=1, device_id=friend, device_id_type=MESH)

    for i in range(2):
        rows = pl.ds(i * 128, 128)
        message[rows, :] = density[rows, :] * pattern[i, 0].astype(jnp.float32)
        message[pl.ds(ROWS + 8 * i, 8), :] = jnp.zeros((8, COLS), jnp.float32) + keep_mask[
            i, 0
        ].astype(jnp.float32)
    pl.semaphore_wait(barrier, len(friends))

    @pl.when(swaps)
    def _():
        swap = pltpu.make_async_remote_copy(
            message, own, swap_sems.at[0], swap_sems.at[1], device_id=across, device_id_type=MESH
        )
        swap.start()
        swap.wait()

    @pl.when(jnp.logical_not(swaps))
    def _():
        own[...] = message[...]

    def split(value):
        high = value.astype(jnp.bfloat16)
        low = (value - high.astype(jnp.float32)).astype(jnp.bfloat16)
        return high, low

    def split_panel(s, zz):
        for i in range(2):
            for j in range(2):
                high, low = split(panel[s, zz * 4 + i * 2 + j])
                left[zz * 2 + i, 0:ROWS, j * 128 : (j + 1) * 128] = high
                left[zz * 2 + i, ROWS : 2 * ROWS, j * 128 : (j + 1) * 128] = low

    def split_column(s, p, g):
        high, low = split(column[s, p, g])
        right[g, :, 0:COLS] = high
        right[g, :, COLS : 2 * COLS] = low

    def multiply(g):
        total[...] += jnp.dot(left[g], right[g], preferred_element_type=jnp.float32)

    def finish(i):
        rows, below = pl.ds(i * 128, 128), pl.ds(ROWS + i * 128, 128)
        one, two = pl.ds(0, COLS), pl.ds(COLS, COLS)
        value = total[rows, one] + (total[rows, two] + total[below, one] + total[below, two])
        return value * own[pl.ds(ROWS + 8 * i, 1), :]

    def step(s, _):
        def send_panel(xx, zz, first, size, half, to):
            part = panel.at[s, slot(xx, zz), pl.ds(first, size)]
            color = first // CUT
            pltpu.make_async_remote_copy(
                part, part, send_sems.at[s, 0], panel_sems.at[s, slot(xx, zz), color * 2 + half],
                device_id=to, device_id_type=MESH,
            ).start()

        def take_panel(xx, zz, first, size, half):
            part = panel.at[s, slot(xx, zz), pl.ds(first, size)]
            arrived(part, panel_sems.at[s, slot(xx, zz), (first // CUT) * 2 + half])

        def send_column(p, cc, yy, first, size, half, to):
            part = column.at[s, p, cc * NY + yy, pl.ds(first, size)]
            pltpu.make_async_remote_copy(
                part, part, send_sems.at[s, 1 + p], column_sems.at[s, p, cc * NY + yy, half],
                device_id=to, device_id_type=MESH,
            ).start()

        def take_column(p, cc, yy, first, size, half):
            part = column.at[s, p, cc * NY + yy, pl.ds(first, size)]
            arrived(part, column_sems.at[s, p, cc * NY + yy, half])

        def wrap(v, n):
            return (v + n) % n

        def column_round(p, d):
            for side in (1, -1):
                yy = wrap(y - side * d, NY)
                half = 0 if side == 1 else 1
                if d < 4:
                    take_column(p, c, yy, 0, ROWS, 0)
                    if d < 3:
                        send_column(p, c, yy, 0, ROWS, 0, at(dy=side))
                    else:
                        send_column(p, c, yy, half * 128, 128, half, at(dy=side))
                    send_column(p, c, yy, 0, ROWS, 0, sibling)
                else:
                    take_column(p, c, yy, half * 128, 128, half)
                    send_column(p, c, yy, half * 128, 128, half, sibling)

        def column_start(p):
            for side in (1, -1):
                send_column(p, c, y, 0, ROWS, 0, at(dy=side))
            send_column(p, c, y, 0, ROWS, 0, sibling)

        def column_other(p, d):
            for side in (1, -1):
                yy = wrap(y - side * d, NY)
                if d < 4:
                    if d > 0 or side == 1:
                        take_column(p, 1 - c, yy, 0, ROWS, 0)
                else:
                    half = 0 if side == 1 else 1
                    take_column(p, 1 - c, yy, half * 128, 128, half)

        def along_x(zz, first, size, half):
            for dx in (2, 1, -1):
                send_panel(x, zz, first, size, half, at(dx=dx))

        def second_round(d):
            for side in (1, -1):
                zz = wrap(z - side * d, NZ)
                half = 0 if side == 1 else 1
                if d < 4:
                    take_panel(x, zz, CUT, 128, 0)
                    if d < 3:
                        send_panel(x, zz, CUT, 128, 0, at(dz=side))
                    else:
                        send_panel(x, zz, CUT + half * 64, 64, half, at(dz=side))
                    along_x(zz, CUT, 128, 0)
                else:
                    take_panel(x, zz, CUT + half * 64, 64, half)
                    along_x(zz, CUT + half * 64, 64, half)

        def first_round(d):
            for dx in (0, 1, -1, 2):
                xx = wrap(x + dx, NX)
                for side in (1, -1):
                    zz = wrap(z - side * d, NZ)
                    half = 0 if side == 1 else 1
                    if d < 4:
                        take_panel(xx, zz, 0, 128, 0)
                        if d < 3:
                            send_panel(xx, zz, 0, 128, 0, at(dz=side))
                        else:
                            send_panel(xx, zz, half * 64, 64, half, at(dz=side))
                    else:
                        take_panel(xx, zz, half * 64, 64, half)

        def panel_ready(d):
            for dx in (1, -1, 2):
                xx = wrap(x + dx, NX)
                for side in (1, -1):
                    zz = wrap(z - side * d, NZ)
                    half = 0 if side == 1 else 1
                    if d == 4:
                        take_panel(xx, zz, CUT + half * 64, 64, half)
                    elif d > 0 or side == 1:
                        take_panel(xx, zz, CUT, 128, 0)
            for side in (1, -1):
                if side == 1 or d in (1, 2, 3):
                    split_panel(s, wrap(z - side * d, NZ))

        def panel_dots(d):
            for side in (1, -1):
                if side == 1 or d in (1, 2, 3):
                    zz = wrap(z - side * d, NZ)
                    for i in range(2):
                        multiply(zz * 2 + i)

        def column_dots(p, cc, d, dots):
            for side in (1, -1):
                if side == 1 or d in (1, 2, 3):
                    g = cc * NY + wrap(y - side * d, NY)
                    split_column(s, p, g)
                    if dots:
                        multiply(g)

        panel[s, slot(x, z)] = own[0:ROWS, :]
        column[s, 0, c * NY + y] = own[0:ROWS, :]
        for side in (1, -1):
            send_panel(x, z, CUT, 128, 0, at(dz=side))
        along_x(z, 0, 128, 0)
        for side in (1, -1):
            send_column(0, c, y, 0, ROWS, 0, at(dy=side))
            send_panel(x, z, 0, 128, 0, at(dz=side))
        along_x(z, CUT, 128, 0)
        send_column(0, c, y, 0, ROWS, 0, sibling)
        total[...] = jnp.zeros_like(total)
        column_dots(0, c, 0, False)

        for dx in (1, -1, 2):
            xx = wrap(x + dx, NX)
            take_panel(xx, z, 0, 128, 0)
            for side in (1, -1):
                send_panel(xx, z, 0, 128, 0, at(dz=side))
        second_round(1)
        column_round(0, 1)
        column_other(0, 0)
        column_dots(0, 1 - c, 0, False)
        column_dots(0, c, 1, False)
        first_round(1)
        column_round(0, 2)
        column_other(0, 1)
        second_round(2)
        column_dots(0, 1 - c, 1, False)
        column_dots(0, c, 2, False)
        panel_ready(0)
        column_round(0, 3)
        column_other(0, 2)
        first_round(2)
        column_dots(0, 1 - c, 2, False)
        column_dots(0, c, 3, False)
        panel_ready(1)
        column_round(0, 4)
        column_other(0, 3)
        second_round(3)
        column_dots(0, 1 - c, 3, False)
        column_dots(0, c, 4, False)
        first_round(3)
        column_other(0, 4)
        column_dots(0, 1 - c, 4, False)
        panel_dots(0)
        panel_dots(1)
        panel_ready(2)
        second_round(4)
        panel_dots(2)
        first_round(4)
        panel_ready(3)
        panel_dots(3)
        panel_ready(4)
        panel_dots(4)

        for i in range(2):
            column[s, 1, c * NY + y, pl.ds(i * 128, 128)] = finish(i)
        column_start(1)
        total[...] = jnp.zeros_like(total)
        column_dots(1, c, 0, True)
        column_round(1, 1)
        column_other(1, 0)
        column_dots(1, 1 - c, 0, True)
        column_dots(1, c, 1, True)
        column_round(1, 2)
        column_other(1, 1)
        column_dots(1, 1 - c, 1, True)
        column_dots(1, c, 2, True)
        column_round(1, 3)
        column_other(1, 2)
        column_dots(1, 1 - c, 2, True)
        column_dots(1, c, 3, True)
        column_round(1, 4)
        column_other(1, 3)
        column_dots(1, 1 - c, 3, True)
        column_dots(1, c, 4, True)
        column_other(1, 4)
        column_dots(1, 1 - c, 4, True)
        for i in range(2):
            rows = pl.ds(i * 128, 128)
            own[rows, :] = 3.0 * column[s, 1, c * NY + y, rows] - 2.0 * finish(i)

        arrived(panel.at[s, pl.ds(0, 31)], send_sems.at[s, 0])
        for p in range(2):
            arrived(column.at[s, p, pl.ds(0, 15)], send_sems.at[s, 1 + p])
        return 0

    lax.fori_loop(0, STEPS, step, 0)

    @pl.when(swaps)
    def _():
        answer[...] = own[0:ROWS, :]
        swap = pltpu.make_async_remote_copy(
            answer, reply, swap_sems.at[2], swap_sems.at[3], device_id=across, device_id_type=MESH
        )
        swap.start()
        swap.wait()
        out[...] = reply[...]

    @pl.when(jnp.logical_not(swaps))
    def _():
        out[...] = own[0:ROWS, :]


def per_device(density, pattern, keep_mask):
    f32, bf16 = jnp.float32, jnp.bfloat16
    return pl.pallas_call(
        kernel,
        out_shape=jax.ShapeDtypeStruct((ROWS, COLS), f32),
        in_specs=[
            pl.BlockSpec(memory_space=pltpu.VMEM),
            pl.BlockSpec(memory_space=pltpu.SMEM),
            pl.BlockSpec(memory_space=pltpu.SMEM),
        ],
        out_specs=pl.BlockSpec(memory_space=pltpu.VMEM),
        scratch_shapes=[
            pltpu.VMEM((ROWS + 16, COLS), f32),
            pltpu.VMEM((ROWS + 16, COLS), f32),
            pltpu.VMEM((STEPS, 32, ROWS, COLS), f32),
            pltpu.VMEM((STEPS, 2, GROUPS, ROWS, COLS), f32),
            pltpu.VMEM((GROUPS, 2 * ROWS, 2 * COLS), bf16),
            pltpu.VMEM((GROUPS, ROWS, 2 * COLS), bf16),
            pltpu.VMEM((2 * ROWS, 2 * COLS), f32),
            pltpu.VMEM((ROWS, COLS), f32),
            pltpu.VMEM((ROWS, COLS), f32),
            pltpu.VMEM((ROWS, COLS), f32),
            pltpu.SemaphoreType.DMA((4,)),
            pltpu.SemaphoreType.DMA((STEPS, 32, 4)),
            pltpu.SemaphoreType.DMA((STEPS, 2, GROUPS, 2)),
            pltpu.SemaphoreType.DMA((STEPS, 3)),
        ],
        compiler_params=pltpu.CompilerParams(
            collective_id=0, has_side_effects=True, vmem_limit_bytes=40 << 20
        ),
        cost_estimate=pl.CostEstimate(
            flops=2 * STEPS * 2 * ROWS * 4096 * COLS, bytes_accessed=1 << 18, transcendentals=0
        ),
    )(density, pattern, keep_mask)


def solution(mesh):
    placed = (P("row", "col"), P("row", "col"), P("row", "col"))
    return jax.shard_map(
        per_device, mesh=mesh, in_specs=placed, out_specs=P("row", "col"), check_vma=False
    )
```

time: 556 us -> 133 us (0.24)
  waiting for transfers between devices: 508 us -> 0 us
  Pallas kernels: 0 us -> 131 us
  matrix products: 27.8 us -> 0 us
  between operations: 13.5 us -> 0.01 us
    all_gather x6 -> x0, waiting for transfers between devices: 507 us -> none  [the longest x2 180 us: per_device(): columns = lax.all_gather(current, 'row', axis=0, tiled=True)]
    pallas_call x0 -> x1, Pallas kernels: none -> 131 us  [per_device(): pl.pallas_call(kernel, out_shape=jax.ShapeDtypeStruct((ROWS, COLS), f32),...]
    dot_general x4 -> x0, matrix products: 27.8 us -> none  [product(): jnp.dot(left, right, precision=lax.Precision.HIGHEST, preferred_element_t...]
  transfers between devices with their start and end apart: 6 -> 0, of which waited for: 6 -> 0; matrix products, arithmetic and copies ran while one was open for 0% -> 0% of each run, Pallas kernels for 0% -> 0%
where the time goes in v1:
time: 133 us
  Pallas kernels  131 us (98%)
  local copies, waits for them, and re-layouts  2.41 us (2%)
    pallas_call x1, Pallas kernels, per_device(): pl.pallas_call(kernel, out_shape=jax.ShapeDtypeStruct((ROWS, COLS), f32),...  131 us

profile of v1, /device:TPU:1, one launch (start us, length us, event | category | flops | bytes accessed | tf_op | source)
XLA Modules:
  0.0 133.3 jit_solution(2606873912718690710)
XLA Ops:
  0.0 0.0 copy-start.1
  0.0 0.8 copy.4.pattern
  0.8 0.0 copy-done.1
  0.8 0.1 copy.5.keep_mask
  0.9 0.0 copy-start
  0.9 0.9 copy-done
  1.8 130.8 %shard_map.37 = f32[256,128]{1,0:T(8,128)S(1)} custom-call(f32[256,128]{1,0:T(8,128)S(1)} %copy-done, s32[2,1]{1,0:T(2,128)S(1)} %copy.4.pattern, s32[2,1]{1,0:T(2,128)S(1)} %copy.5.keep_mask), custom_call_target="tpu_custom_call" | custom-call | flops 1073741824 | bytes 262144 | tf_op jit(solution)/shard_map/pallas_call | solution.py:327
  132.6 0.7 copy.7
Async XLA Ops:
  0.0 0.8 copy-start.1
  0.9 0.9 copy-start

commit v2 on v0

v2 whole, which is shorter than its diff:
```python
import jax
import jax.numpy as jnp
from jax import lax
from jax.experimental import pallas as pl
from jax.experimental.pallas import tpu as pltpu
from jax.sharding import PartitionSpec as P

STEPS = 2
NX, NY, NZ = 4, 8, 8
RING = 8
ROWS, COLS = 256, 128
GROUPS = 16
FIRST = (192, 192, 128)
MESH = pl.DeviceIdType.MESH
PANEL, COLUMN, SQUARE = 0, 1, 2


def pieces(first):
    half, rest = first // 2, (ROWS - first) // 2
    cut = [(0, half, True, 1), (half, half, True, -1)]
    if rest:
        cut += [(first, rest, False, 1), (first + rest, rest, False, -1)]
    return cut


def place(x, y, z, c):
    return ((x // 2) * NY + y, z * 4 + (x % 2) * 2 + c)


def arrived(ref, sem):
    pltpu.make_async_copy(ref, ref, sem).wait()


def kernel(
    density, pattern, keep_mask, out,
    own, panel, column, left, right, total, panel_sems, column_sems, send_sems,
):
    row, col = lax.axis_index("row"), lax.axis_index("col")
    y, z, c = row % NY, col // 4, col % 2
    h, l = row // NY, (col // 2) % 2
    x = h * 2 + l

    def at(dx=0, dy=0, dz=0, core=None):
        return place(
            (x + dx + NX) % NX, (y + dy + NY) % NY, (z + dz + NZ) % NZ, c if core is None else core
        )

    sibling = at(core=1 - c)
    across = at(dx=2)
    beside = at(dx=1 - 2 * l)
    barrier = pltpu.get_barrier_semaphore()
    friends = [across, beside, at(dy=1), at(dy=-1), at(dz=1), at(dz=-1), sibling]
    for friend in friends:
        pl.semaphore_signal(barrier, inc=1, device_id=friend, device_id_type=MESH)
    for i in range(2):
        rows = pl.ds(i * 128, 128)
        own[rows, :] = density[rows, :] * pattern[i, 0].astype(jnp.float32)
    pl.semaphore_wait(barrier, len(friends))

    def split(value):
        high = value.astype(jnp.bfloat16)
        low = (value - high.astype(jnp.float32)).astype(jnp.bfloat16)
        return high, low

    def finish(i):
        rows, below = pl.ds(i * 128, 128), pl.ds(ROWS + i * 128, 128)
        one, two = pl.ds(0, COLS), pl.ds(COLS, COLS)
        value = total[rows, one] + (total[rows, two] + total[below, one] + total[below, two])
        return value * keep_mask[i, 0].astype(jnp.float32)

    def multiply(g):
        total[...] += jnp.dot(left[g], right[g], preferred_element_type=jnp.float32)

    def step(s, _):
        def slot(kind, w, pos, core):
            if kind == PANEL:
                return pos * 4 + (l if w == 0 else 1 - l) * 2 + core
            return (h if w == 0 else 1 - h) * NY + pos

        def place_of(kind, w, pos, piece, core):
            first, size, _, _ = piece
            n = slot(kind, w, pos, core)
            k = pieces(FIRST[kind]).index(piece)
            if kind == PANEL:
                return panel.at[s, n, pl.ds(first, size)], panel_sems.at[s, n, k]
            return column.at[s, kind - 1, n, pl.ds(first, size)], column_sems.at[s, kind - 1, n, k]

        def send(kind, w, pos, piece, to):
            part, sem = place_of(kind, w, pos, piece, c)
            pltpu.make_async_remote_copy(
                part, part, send_sems.at[s, kind], sem, device_id=to, device_id_type=MESH
            ).start()

        def take(kind, w, pos, piece, core):
            arrived(*place_of(kind, w, pos, piece, core))

        def me(kind):
            return z if kind == PANEL else y

        def pos_of(kind, d, side):
            return (me(kind) - side * d + RING) % RING

        def onward(kind, side):
            return at(dz=side) if kind == PANEL else at(dy=side)

        def partner(kind):
            return beside if kind == PANEL else across

        def share(kind, w, pos, piece):
            if kind == PANEL:
                send(kind, w, pos, piece, sibling)

        def begin(kind):
            cut = pieces(FIRST[kind])
            for piece in cut:
                if piece[2]:
                    send(kind, 0, me(kind), piece, partner(kind))
            for piece in cut[::-1]:
                for side in (1, -1):
                    send(kind, 0, me(kind), piece, onward(kind, side))

        def begin_late(kind):
            for piece in pieces(FIRST[kind]):
                if not piece[2]:
                    send(kind, 0, me(kind), piece, partner(kind))

        def from_partner(kind):
            for piece in pieces(FIRST[kind]):
                if piece[2]:
                    take(kind, 1, me(kind), piece, c)
                    for side in (1, -1):
                        send(kind, 1, me(kind), piece, onward(kind, side))
                    share(kind, 1, me(kind), piece)

        def ring(kind, w, d):
            cut = pieces(FIRST[kind])
            for piece in cut[::-1] if w == 0 else cut[:2]:
                for side in (1, -1):
                    pos = pos_of(kind, d, side)
                    far = side == piece[3]
                    if d < 4 or far:
                        take(kind, w, pos, piece, c)
                        if d < 3 or (d == 3 and far):
                            send(kind, w, pos, piece, onward(kind, side))
                        if not piece[2]:
                            send(kind, w, pos, piece, partner(kind))
                        share(kind, w, pos, piece)

        def sides(d):
            return (1, -1) if d in (1, 2, 3) else (1,)

        def exchanged(kind, d):
            for piece in pieces(FIRST[kind])[2:]:
                for side in sides(d):
                    pos = pos_of(kind, d, side)
                    take(kind, 1, pos, piece, c)
                    share(kind, 1, pos, piece)

        def shared(d):
            for w in range(2):
                for side in sides(d):
                    for piece in pieces(FIRST[PANEL]):
                        take(PANEL, w, pos_of(PANEL, d, side), piece, 1 - c)

        def split_panel(d):
            for side in sides(d):
                zz = pos_of(PANEL, d, side)
                for i in range(2):
                    for j in range(2):
                        high, low = split(panel[s, zz * 4 + i * 2 + j])
                        left[zz * 2 + i, 0:ROWS, j * COLS : (j + 1) * COLS] = high
                        left[zz * 2 + i, ROWS : 2 * ROWS, j * COLS : (j + 1) * COLS] = low

        def split_column(kind, w, d, dots):
            for side in sides(d):
                g = slot(kind, w, pos_of(kind, d, side), c)
                high, low = split(column[s, kind - 1, g])
                right[g, :, 0:COLS] = high
                right[g, :, COLS : 2 * COLS] = low
                if dots:
                    multiply(g)

        def distance(a, b):
            apart = (a - b + RING) % RING
            return jnp.minimum(apart, RING - apart)

        def dots(low, high):
            def one(g, _):
                last = jnp.maximum(distance(g // 2, z), distance(g % NY, y))

                @pl.when(jnp.logical_and(last >= low, last <= high))
                def _():
                    multiply(g)

                return 0

            lax.fori_loop(0, GROUPS, one, 0)

        both = (PANEL, COLUMN)
        panel[s, col] = own[...]
        column[s, 0, row] = own[...]
        for kind in both:
            begin(kind)
        for piece in pieces(FIRST[PANEL]):
            share(PANEL, 0, z, piece)
        total[...] = jnp.zeros_like(total)
        split_column(COLUMN, 0, 0, False)

        def each(function, *args):
            for kind in both:
                function(kind, *args)

        each(ring, 0, 1)
        each(from_partner)
        each(begin_late)
        split_column(COLUMN, 0, 1, False)
        each(ring, 0, 2)
        each(ring, 1, 1)
        each(exchanged, 0)
        each(exchanged, 1)
        split_column(COLUMN, 1, 0, False)
        split_column(COLUMN, 1, 1, False)
        shared(0)
        split_panel(0)
        each(ring, 0, 3)
        each(ring, 1, 2)
        each(exchanged, 2)
        split_column(COLUMN, 0, 2, False)
        split_column(COLUMN, 1, 2, False)
        shared(1)
        split_panel(1)
        each(ring, 0, 4)
        each(ring, 1, 3)
        each(exchanged, 3)
        split_column(COLUMN, 0, 3, False)
        split_column(COLUMN, 1, 3, False)
        shared(2)
        split_panel(2)
        dots(0, 2)
        each(ring, 1, 4)
        each(exchanged, 4)
        split_column(COLUMN, 0, 4, False)
        shared(3)
        split_panel(3)
        dots(3, 3)
        split_column(COLUMN, 1, 4, False)
        shared(4)
        split_panel(4)
        dots(4, 4)

        for i in range(2):
            column[s, 1, row, pl.ds(i * 128, 128)] = finish(i)
        begin(SQUARE)
        total[...] = jnp.zeros_like(total)
        split_column(SQUARE, 0, 0, True)
        ring(SQUARE, 0, 1)
        from_partner(SQUARE)
        begin_late(SQUARE)
        split_column(SQUARE, 0, 1, True)
        ring(SQUARE, 0, 2)
        ring(SQUARE, 1, 1)
        exchanged(SQUARE, 0)
        exchanged(SQUARE, 1)
        split_column(SQUARE, 1, 0, True)
        split_column(SQUARE, 1, 1, True)
        ring(SQUARE, 0, 3)
        ring(SQUARE, 1, 2)
        exchanged(SQUARE, 2)
        split_column(SQUARE, 0, 2, True)
        split_column(SQUARE, 1, 2, True)
        ring(SQUARE, 0, 4)
        ring(SQUARE, 1, 3)
        exchanged(SQUARE, 3)
        split_column(SQUARE, 0, 3, True)
        split_column(SQUARE, 1, 3, True)
        split_column(SQUARE, 0, 4, True)
        ring(SQUARE, 1, 4)
        exchanged(SQUARE, 4)
        split_column(SQUARE, 1, 4, True)
        for i in range(2):
            rows = pl.ds(i * 128, 128)
            own[rows, :] = 3.0 * column[s, 1, row, rows] - 2.0 * finish(i)

        arrived(panel.at[s, pl.ds(0, 31)], send_sems.at[s, PANEL])
        for p in range(2):
            arrived(column.at[s, p, pl.ds(0, 15)], send_sems.at[s, 1 + p])
        return 0

    lax.fori_loop(0, STEPS, step, 0)
    out[...] = own[...]


def per_device(density, pattern, keep_mask):
    f32, bf16 = jnp.float32, jnp.bfloat16
    return pl.pallas_call(
        kernel,
        out_shape=jax.ShapeDtypeStruct((ROWS, COLS), f32),
        in_specs=[
            pl.BlockSpec(memory_space=pltpu.VMEM),
            pl.BlockSpec(memory_space=pltpu.SMEM),
            pl.BlockSpec(memory_space=pltpu.SMEM),
        ],
        out_specs=pl.BlockSpec(memory_space=pltpu.VMEM),
        scratch_shapes=[
            pltpu.VMEM((ROWS, COLS), f32),
            pltpu.VMEM((STEPS, 32, ROWS, COLS), f32),
            pltpu.VMEM((STEPS, 2, GROUPS, ROWS, COLS), f32),
            pltpu.VMEM((GROUPS, 2 * ROWS, 2 * COLS), bf16),
            pltpu.VMEM((GROUPS, ROWS, 2 * COLS), bf16),
            pltpu.VMEM((2 * ROWS, 2 * COLS), f32),
            pltpu.SemaphoreType.DMA((STEPS, 32, 4)),
            pltpu.SemaphoreType.DMA((STEPS, 2, GROUPS, 4)),
            pltpu.SemaphoreType.DMA((STEPS, 3)),
        ],
        compiler_params=pltpu.CompilerParams(
            collective_id=0, has_side_effects=True, vmem_limit_bytes=40 << 20
        ),
        cost_estimate=pl.CostEstimate(
            flops=2 * STEPS * 2 * ROWS * 4096 * COLS, bytes_accessed=1 << 18, transcendentals=0
        ),
    )(density, pattern, keep_mask)


def solution(mesh):
    placed = (P("row", "col"), P("row", "col"), P("row", "col"))
    return jax.shard_map(
        per_device, mesh=mesh, in_specs=placed, out_specs=P("row", "col"), check_vma=False
    )
```

time: 556 us -> 118 us (0.21)
  the two profiles are of different devices: /device:TPU:1 before, /device:TPU:16 now
where the time goes in v2:
time: 118 us
  Pallas kernels  115 us (97%)
  local copies, waits for them, and re-layouts  2.41 us (2%)
    pallas_call x1, Pallas kernels, per_device(): pl.pallas_call(kernel, out_shape=jax.ShapeDtypeStruct((ROWS, COLS), f32),...  115 us
    unnamed x7, local copies, waits for them, and re-layouts  2.41 us

profile of v2, /device:TPU:16, one launch (start us, length us, event | category | flops | bytes accessed | tf_op | source)
XLA Modules:
  0.0 117.7 jit_solution(18436733782995843246)
XLA Ops:
  0.0 0.0 copy-start.1
  0.0 0.8 copy.4.pattern
  0.8 0.0 copy-done.1
  0.8 0.1 copy.5.keep_mask
  0.9 0.0 copy-start
  0.9 0.9 copy-done
  1.8 115.2 %shard_map.37 = f32[256,128]{1,0:T(8,128)S(1)} custom-call(f32[256,128]{1,0:T(8,128)S(1)} %copy-done, s32[2,1]{1,0:T(2,128)S(1)} %copy.4.pattern, s32[2,1]{1,0:T(2,128)S(1)} %copy.5.keep_mask), custom_call_target="tpu_custom_call" | custom-call | flops 1073741824 | bytes 262144 | tf_op jit(solution)/shard_map/pallas_call | solution.py:295
  117.0 0.7 copy.7
Async XLA Ops:
  0.0 0.8 copy-start.1
  0.9 0.9 copy-start

commit v3 on v0

v3 whole, which is shorter than its diff:
```python
import functools

import jax
import jax.numpy as jnp
from jax import lax
from jax.experimental import pallas as pl
from jax.experimental.pallas import tpu as pltpu
from jax.sharding import PartitionSpec as P

STEPS = 2
NX, NY, NZ = 4, 8, 8
RING = 8
ROWS, COLS = 256, 128
GROUPS = 16
MESH = pl.DeviceIdType.MESH
PANEL, COLUMN, SQUARE = 0, 1, 2
CHUNK = 64
MOST = ((False, 1), (True, -1), (True, 1), (True, -1))
HALF = ((False, 1), (False, -1), (True, 1), (True, -1))
ROUTES = (MOST, MOST, HALF)


def place(x, y, z, c):
    return ((x // 2) * NY + y, z * 4 + (x % 2) * 2 + c)


def arrived(ref, sem):
    pltpu.make_async_copy(ref, ref, sem).wait()


def kernel(
    density, pattern, keep_mask, out,
    own, panel, column, left, right, total, panel_sems, column_sems, send_sems, load_sem,
):
    row, col = lax.axis_index("row"), lax.axis_index("col")
    y, z, c = row % NY, col // 4, col % 2
    h, l = row // NY, (col // 2) % 2
    x = h * 2 + l

    def at(dx=0, dy=0, dz=0, core=None):
        return place(
            (x + dx + NX) % NX, (y + dy + NY) % NY, (z + dz + NZ) % NZ, c if core is None else core
        )

    sibling = at(core=1 - c)
    across = at(dx=2)
    beside = at(dx=1 - 2 * l)
    barrier = pltpu.get_barrier_semaphore()
    friends = [across, beside, at(dy=1), at(dy=-1), at(dz=1), at(dz=-1), sibling]
    for friend in friends:
        pl.semaphore_signal(barrier, inc=1, device_id=friend, device_id_type=MESH)
    load = pltpu.make_async_copy(density, own, load_sem)
    load.start()
    pl.semaphore_wait(barrier, len(friends))
    load.wait()
    for i in range(2):
        rows = pl.ds(i * 128, 128)
        own[rows, :] *= pattern[0, i].astype(jnp.float32)

    def split(value):
        high = value.astype(jnp.bfloat16)
        low = (value - high.astype(jnp.float32)).astype(jnp.bfloat16)
        return high, low

    def rows_of(r):
        return pl.ds(r * CHUNK, CHUNK)

    def multiply(g):
        both = left[g].reshape(2 * ROWS, 2 * COLS)
        total[...] += jnp.dot(both, right[g], preferred_element_type=jnp.float32)

    def clear():
        total[...] = jnp.zeros_like(total)

    def product(r, groups, begun):
        both = total[pl.ds(r * 2 * CHUNK, 2 * CHUNK), :] if begun else 0.0
        for g in groups:
            both += jnp.dot(left[g, r], right[g], preferred_element_type=jnp.float32)
        high, low = both[0:CHUNK], both[CHUNK : 2 * CHUNK]
        value = high[:, 0:COLS] + (high[:, COLS : 2 * COLS] + low[:, 0:COLS] + low[:, COLS : 2 * COLS])
        return value * keep_mask[0, r // 2].astype(jnp.float32)

    def slot(kind, w, pos, core):
        if kind == PANEL:
            return pos * 4 + (l if w == 0 else 1 - l) * 2 + core
        return (h if w == 0 else 1 - h) * NY + pos

    def place_of(s, kind, w, pos, r, core):
        n = slot(kind, w, pos, core)
        if kind == PANEL:
            return panel.at[s, n, rows_of(r)], panel_sems.at[s, n, r]
        return column.at[s, kind - 1, n, rows_of(r)], column_sems.at[s, kind - 1, n, r]

    def send(s, kind, w, pos, r, to):
        part, sem = place_of(s, kind, w, pos, r, c)
        pltpu.make_async_remote_copy(
            part, part, send_sems.at[s, kind], sem, device_id=to, device_id_type=MESH
        ).start()

    def me(kind):
        return z if kind == PANEL else y

    def onward(kind, side):
        return at(dz=side) if kind == PANEL else at(dy=side)

    def partner(kind):
        return beside if kind == PANEL else across

    def share(s, kind, w, pos, r):
        if kind == PANEL:
            send(s, kind, w, pos, r, sibling)

    def launch(s, kind, r):
        along_x, far = ROUTES[kind][r]
        send(s, kind, 0, me(kind), r, onward(kind, far))
        if along_x:
            send(s, kind, 0, me(kind), r, partner(kind))
        send(s, kind, 0, me(kind), r, onward(kind, -far))
        share(s, kind, 0, me(kind), r)

    def launch_current(s, r):
        panel[s, col, rows_of(r)] = own[rows_of(r), :]
        column[s, 0, row, rows_of(r)] = own[rows_of(r), :]
        launch(s, PANEL, r)
        launch(s, COLUMN, r)

    for r in range(4):
        launch_current(0, r)

    def step(s, _):
        def take(kind, w, pos, r, core):
            arrived(*place_of(s, kind, w, pos, r, core))

        def pos_of(kind, d, side):
            return (me(kind) - side * d + RING) % RING

        def late(kind):
            for r in range(4):
                if not ROUTES[kind][r][0]:
                    send(s, kind, 0, me(kind), r, partner(kind))

        def sides(d):
            return (1, -1) if d in (1, 2, 3) else (1,)

        def ring(kind, w, d, r):
            along_x, far = ROUTES[kind][r]
            if d == 0:
                take(kind, w, me(kind), r, c)
                for side in (far, -far):
                    send(s, kind, w, me(kind), r, onward(kind, side))
                share(s, kind, w, me(kind), r)
                return
            for side in (far, -far):
                pos = pos_of(kind, d, side)
                if d < 4 or side == far:
                    take(kind, w, pos, r, c)
                    if d < 3 or (d == 3 and side == far):
                        send(s, kind, w, pos, r, onward(kind, side))
                    if not along_x:
                        send(s, kind, w, pos, r, partner(kind))
                    share(s, kind, w, pos, r)

        def turn(kinds, d, work=()):
            work = list(work)
            for r in range(4):
                for kind in kinds:
                    if d <= 4:
                        ring(kind, 0, d, r)
                    if ROUTES[kind][r][0]:
                        ring(kind, 1, d - 1, r)
                    if work:
                        work.pop(0)()
            for unit in work:
                unit()
            if d == 1:
                for kind in kinds:
                    late(kind)

        def exchanged(kinds, d):
            for r in range(4):
                for kind in kinds:
                    if not ROUTES[kind][r][0]:
                        for side in sides(d):
                            pos = pos_of(kind, d, side)
                            take(kind, 1, pos, r, c)
                            share(s, kind, 1, pos, r)

        def shared(d):
            for w in range(2):
                for side in sides(d):
                    for r in range(4):
                        take(PANEL, w, pos_of(PANEL, d, side), r, 1 - c)

        def split_block(zz, i, j):
            high, low = split(panel[s, zz * 4 + i * 2 + j])
            for r in range(4):
                rows = slice(r * CHUNK, (r + 1) * CHUNK)
                left[zz * 2 + i, r, 0:CHUNK, j * COLS : (j + 1) * COLS] = high[rows]
                left[zz * 2 + i, r, CHUNK : 2 * CHUNK, j * COLS : (j + 1) * COLS] = low[rows]

        def panel_work(d):
            return [
                functools.partial(split_block, pos_of(PANEL, d, side), i, j)
                for side in sides(d) for i in range(2) for j in range(2)
            ]

        def column_work(kind, w, d):
            return [functools.partial(split_one, kind, w, d, side) for side in sides(d)]

        def run(work):
            for unit in work:
                unit()

        def split_one(kind, w, d, side):
            g = slot(kind, w, pos_of(kind, d, side), c)
            high, low = split(column[s, kind - 1, g])
            right[g, :, 0:COLS] = high
            right[g, :, COLS : 2 * COLS] = low
            if kind == SQUARE and d < 4:
                multiply(g)

        both = (PANEL, COLUMN)
        turn(both, 1, column_work(COLUMN, 0, 0))
        turn(both, 2, column_work(COLUMN, 0, 1))
        exchanged(both, 0)
        shared(0)
        turn(both, 3, panel_work(0) + column_work(COLUMN, 0, 2) + column_work(COLUMN, 1, 0))
        exchanged(both, 1)
        shared(1)
        turn(both, 4, panel_work(1) + column_work(COLUMN, 1, 1))
        exchanged(both, 2)
        shared(2)
        turn(both, 5, panel_work(2) + column_work(COLUMN, 0, 3) + column_work(COLUMN, 1, 2))
        exchanged(both, 3)
        run(column_work(COLUMN, 0, 4) + column_work(COLUMN, 1, 3))
        exchanged(both, 4)
        shared(3)
        run(panel_work(3) + column_work(COLUMN, 1, 4))
        shared(4)
        run(panel_work(4))

        for r in range(4):
            column[s, 1, row, rows_of(r)] = product(r, range(GROUPS), False)
            launch(s, SQUARE, r)
        only = (SQUARE,)
        clear()
        turn(only, 1, column_work(SQUARE, 0, 0))
        turn(only, 2, column_work(SQUARE, 0, 1))
        exchanged(only, 0)
        turn(only, 3, column_work(SQUARE, 0, 2) + column_work(SQUARE, 1, 0))
        exchanged(only, 1)
        turn(only, 4, column_work(SQUARE, 0, 3) + column_work(SQUARE, 1, 1))
        exchanged(only, 2)
        turn(only, 5, column_work(SQUARE, 1, 2))
        exchanged(only, 3)
        run(column_work(SQUARE, 1, 3) + column_work(SQUARE, 0, 4))
        exchanged(only, 4)
        run(column_work(SQUARE, 1, 4))
        last = [slot(SQUARE, w, pos_of(SQUARE, 4, 1), c) for w in range(2)]
        for r in range(4):
            own[rows_of(r), :] = 3.0 * column[s, 1, row, rows_of(r)] - 2.0 * product(r, last, True)

            @pl.when(s + 1 < STEPS)
            def _():
                launch_current(s + 1, r)

        arrived(panel.at[s, pl.ds(0, 31)], send_sems.at[s, PANEL])
        for p in range(2):
            arrived(column.at[s, p, pl.ds(0, 15)], send_sems.at[s, 1 + p])
        return 0

    lax.fori_loop(0, STEPS, step, 0)
    out[...] = own[...]


def per_device(density, pattern, keep_mask):
    f32, bf16 = jnp.float32, jnp.bfloat16
    return pl.pallas_call(
        kernel,
        out_shape=jax.ShapeDtypeStruct((ROWS, COLS), f32),
        in_specs=[
            pl.BlockSpec(memory_space=pltpu.HBM),
            pl.BlockSpec(memory_space=pltpu.SMEM),
            pl.BlockSpec(memory_space=pltpu.SMEM),
        ],
        out_specs=pl.BlockSpec(memory_space=pltpu.VMEM),
        scratch_shapes=[
            pltpu.VMEM((ROWS, COLS), f32),
            pltpu.VMEM((STEPS, 32, ROWS, COLS), f32),
            pltpu.VMEM((STEPS, 2, GROUPS, ROWS, COLS), f32),
            pltpu.VMEM((GROUPS, 4, 2 * CHUNK, 2 * COLS), bf16),
            pltpu.VMEM((GROUPS, ROWS, 2 * COLS), bf16),
            pltpu.VMEM((2 * ROWS, 2 * COLS), f32),
            pltpu.SemaphoreType.DMA((STEPS, 32, 4)),
            pltpu.SemaphoreType.DMA((STEPS, 2, GROUPS, 4)),
            pltpu.SemaphoreType.DMA((STEPS, 3)),
            pltpu.SemaphoreType.DMA,
        ],
        compiler_params=pltpu.CompilerParams(
            collective_id=0, has_side_effects=True, vmem_limit_bytes=40 << 20
        ),
        cost_estimate=pl.CostEstimate(
            flops=2 * STEPS * 2 * ROWS * 4096 * COLS, bytes_accessed=1 << 18, transcendentals=0
        ),
    )(density, pattern.T, keep_mask.T)


def solution(mesh):
    placed = (P("row", "col"), P("row", "col"), P("row", "col"))
    return jax.shard_map(
        per_device, mesh=mesh, in_specs=placed, out_specs=P("row", "col"), check_vma=False
    )
```

time: 556 us -> 111 us (0.20)
  waiting for transfers between devices: 508 us -> 0 us
  Pallas kernels: 0 us -> 109 us
  matrix products: 27.8 us -> 0 us
  between operations: 13.5 us -> 0.01 us
    all_gather x6 -> x0, waiting for transfers between devices: 507 us -> none  [the longest x2 180 us: per_device(): columns = lax.all_gather(current, 'row', axis=0, tiled=True)]
    pallas_call x0 -> x1, Pallas kernels: none -> 109 us  [per_device(): pl.pallas_call(kernel, out_shape=jax.ShapeDtypeStruct((ROWS, COLS), f32),...]
    dot_general x4 -> x0, matrix products: 27.8 us -> none  [product(): jnp.dot(left, right, precision=lax.Precision.HIGHEST, preferred_element_t...]
  transfers between devices with their start and end apart: 6 -> 0, of which waited for: 6 -> 0; matrix products, arithmetic and copies ran while one was open for 0% -> 0% of each run, Pallas kernels for 0% -> 0%
where the time goes in v3:
time: 111 us
  Pallas kernels  109 us (98%)
  local copies, waits for them, and re-layouts  2.23 us (2%)
    pallas_call x1, Pallas kernels, per_device(): pl.pallas_call(kernel, out_shape=jax.ShapeDtypeStruct((ROWS, COLS), f32),...  109 us
    unnamed x7, local copies, waits for them, and re-layouts  2.23 us

profile of v3, /device:TPU:1, one launch (start us, length us, event | category | flops | bytes accessed | tf_op | source)
XLA Modules:
  0.0 111.3 jit_solution(9036873842674633874)
XLA Ops:
  0.0 0.0 copy-start.1
  0.0 0.0 copy-start.2
  0.0 0.7 copy-done.1
  0.7 0.0 copy-done.2
  0.7 0.0 copy-start
  0.7 0.9 copy-done
  1.6 109.0 %shard_map.37 = f32[256,128]{1,0:T(8,128)S(1)} custom-call(f32[256,128]{1,0:T(8,128)S(1)} %copy-done, s32[1,2]{1,0:T(1,128)S(1)} %bitcast.2, s32[1,2]{1,0:T(1,128)S(1)} %bitcast.3), custom_call_target="tpu_custom_call" | custom-call | flops 1073741824 | bytes 262144 | tf_op jit(solution)/shard_map/pallas_call | solution.py:278
  110.6 0.7 copy.5
Async XLA Ops:
  0.0 0.7 copy-start.1
  0.0 0.7 copy-start.2
  0.7 0.9 copy-start

commit v4 on v3

--- a/solution.py
+++ b/solution.py
@@ -166,6 +166,7 @@
                 for kind in kinds:
                     if d <= 4:
                         ring(kind, 0, d, r)
+                for kind in kinds:
                     if ROUTES[kind][r][0]:
                         ring(kind, 1, d - 1, r)
                     if work:
@@ -216,7 +217,7 @@
             high, low = split(column[s, kind - 1, g])
             right[g, :, 0:COLS] = high
             right[g, :, COLS : 2 * COLS] = low
-            if kind == SQUARE and d < 4:
+            if kind == SQUARE and d < 3:
                 multiply(g)
 
         both = (PANEL, COLUMN)
@@ -256,7 +257,7 @@
         run(column_work(SQUARE, 1, 3) + column_work(SQUARE, 0, 4))
         exchanged(only, 4)
         run(column_work(SQUARE, 1, 4))
-        last = [slot(SQUARE, w, pos_of(SQUARE, 4, 1), c) for w in range(2)]
+        last = [slot(SQUARE, w, pos_of(SQUARE, d, side), c) for d in range(3, 5) for side in sides(d) for w in range(2)]
         for r in range(4):
             own[rows_of(r), :] = 3.0 * column[s, 1, row, rows_of(r)] - 2.0 * product(r, last, True)
 

time: 111 us -> 112 us (level)
  no operation moved by 1% of the time
where the time goes in v4:
time: 112 us
  Pallas kernels  109 us (97%)
  local copies, waits for them, and re-layouts  2.23 us (2%)
    pallas_call x1, Pallas kernels, per_device(): pl.pallas_call(kernel, out_shape=jax.ShapeDtypeStruct((ROWS, COLS), f32),...  109 us

profile of v4, /device:TPU:1, one launch (start us, length us, event | category | flops | bytes accessed | tf_op | source)
XLA Modules:
  0.0 111.5 jit_solution(2141547516925597092)
XLA Ops:
  0.0 0.0 copy-start.1
  0.0 0.0 copy-start.2
  0.0 0.7 copy-done.1
  0.7 0.0 copy-done.2
  0.7 0.0 copy-start
  0.7 0.9 copy-done
  1.6 109.3 %shard_map.37 = f32[256,128]{1,0:T(8,128)S(1)} custom-call(f32[256,128]{1,0:T(8,128)S(1)} %copy-done, s32[1,2]{1,0:T(1,128)S(1)} %bitcast.2, s32[1,2]{1,0:T(1,128)S(1)} %bitcast.3), custom_call_target="tpu_custom_call" | custom-call | flops 1073741824 | bytes 262144 | tf_op jit(solution)/shard_map/pallas_call | solution.py:279
  110.8 0.7 copy.5
Async XLA Ops:
  0.0 0.7 copy-start.1
  0.0 0.7 copy-start.2
  0.7 0.9 copy-start
